TPU v7x, 256 devices: a whole 4x4x8 slice. The times are simulated.
256 devices in a mesh: seq: 16 (over z, y_hi), head: 16 (over x, y_lo, core).
Axes of the slice: x: 4, y: 4 (y_hi: 2, y_lo: 2; y = y_hi * 2 + y_lo), z: 8, core: 2. Of those that a mesh axis runs over, the one named last changes fastest.
Arguments:
- queries: bfloat16 [16384, 4096], P('seq', 'head'), may hold values from -40 to 40
- keys: bfloat16 [16384, 4096], P('seq', 'head'), may hold values from -6 to 6
- values: bfloat16 [16384, 4096], P('seq', 'head'), may hold values from -6 to 6
- out_weight: bfloat16 [4096, 4096], P('head'), may hold values from -0.125 to 0.125
- band_mask: int32 [32, 3], P('seq'), may hold values 0 or 1
- summary_positions: int32 [1024], replicated, may hold values from 0 to 16383, as said below
Outputs:
- mixed: bfloat16 [16384, 4096], P('seq', 'head')
- summary: bfloat16 [1024, 4096], P('seq', 'head')
Inputs may be any that keep to these rules, and one draw needn't show every extreme that they name: `summary_positions`: 1024 distinct positions in ascending order; positions 0 and 16383 are always among them.
All inputs are finite; a program needn't handle non-finite values. No bound on the sum of `band_mask` on one device may be relied on, other than what follows from the above.
Results may differ from a plain program's by a relative error of at most 0.0057.
Values may be sent and summed in bfloat16 or wider, within the bound.
No kernel may reach another device: no remote copies, remote signals or barrier semaphores. Data moves between devices by JAX's collectives and lax.ppermute only.
A program may use at most 128 MiB of HBM per device.

v0:
```python
import math

import jax
import jax.numpy as jnp
from jax import lax
from jax.sharding import PartitionSpec as P

HEAD_DIM = 128
BLOCK = 512


def extended(cells, sides, width):
    for axis, dim in sides:
        count = lax.axis_size(axis)
        ends = count - 1
        head = lax.slice_in_dim(cells, 0, width, axis=dim)
        tail = lax.slice_in_dim(cells, cells.shape[dim] - width, cells.shape[dim], axis=dim)
        cells = jnp.concatenate(
            [
                lax.ppermute(tail, axis, [(i, (i + 1) % count) for i in range(ends)]),
                cells,
                lax.ppermute(head, axis, [((i + 1) % count, i) for i in range(ends)]),
            ],
            axis=dim,
        )
    return cells


def band_block(
    query_rows, band_keys, band_values, band_live, summary_keys, summary_values, global_live, scale
):
    count = query_rows.shape[0]
    heads_here = query_rows.shape[1] // HEAD_DIM
    globals_all = summary_keys.shape[0]
    query_heads = query_rows.reshape(count, heads_here, HEAD_DIM)
    global_key_heads = summary_keys.reshape(globals_all, heads_here, HEAD_DIM)
    global_value_heads = summary_values.reshape(globals_all, heads_here, HEAD_DIM)
    global_scores = (
        jnp.einsum(
            "qhd,khd->hqk", query_heads, global_key_heads, preferred_element_type=jnp.float32
        )
        * scale
    )
    global_scores = jnp.where(global_live[None, None, :], global_scores, -jnp.inf)
    key_heads = band_keys.reshape(3 * BLOCK, heads_here, HEAD_DIM)
    value_heads = band_values.reshape(3 * BLOCK, heads_here, HEAD_DIM)
    band_scores = (
        jnp.einsum("qhd,khd->hqk", query_heads, key_heads, preferred_element_type=jnp.float32)
        * scale
    )
    band_scores = jnp.where(jnp.repeat(band_live, BLOCK)[None, None, :], band_scores, -jnp.inf)
    peak = jnp.maximum(jnp.max(band_scores, axis=-1), jnp.max(global_scores, axis=-1))
    band_weights = jnp.exp(band_scores - peak[:, :, None])
    global_weights = jnp.exp(global_scores - peak[:, :, None])
    totals = jnp.sum(band_weights, axis=-1) + jnp.sum(global_weights, axis=-1)
    band_probs = band_weights.astype(jnp.bfloat16)
    global_probs = global_weights.astype(jnp.bfloat16)
    summed = jnp.einsum(
        "hqk,khd->qhd", global_probs, global_value_heads, preferred_element_type=jnp.float32
    )
    summed = summed + jnp.einsum(
        "hqk,khd->qhd", band_probs, value_heads, preferred_element_type=jnp.float32
    )
    result = summed / jnp.transpose(totals)[:, :, None]
    return result.reshape(count, heads_here * HEAD_DIM).astype(jnp.bfloat16)


def per_device(queries, keys, values, out_weight, band_mask, summary_positions):
    tok_rows, width = queries.shape
    heads_here = width // HEAD_DIM
    blocks_here = tok_rows // BLOCK
    seq_count = lax.axis_size("seq")
    seq_rank = lax.axis_index("seq")
    first_token = seq_rank * tok_rows
    total_blocks = seq_count * blocks_here
    globals_all = summary_positions.shape[0]
    glob_rows = globals_all // seq_count
    scale = jnp.float32(1.0 / math.sqrt(HEAD_DIM))
    local_place = summary_positions - first_token
    owned = (local_place >= 0) & (local_place < tok_rows)
    picked_index = jnp.clip(local_place, 0, tok_rows - 1)
    picked_queries = jnp.where(owned[:, None], jnp.take(queries, picked_index, axis=0), 0)
    picked_keys = jnp.where(owned[:, None], jnp.take(keys, picked_index, axis=0), 0)
    picked_values = jnp.where(owned[:, None], jnp.take(values, picked_index, axis=0), 0)
    gathered = (
        lax.psum(picked_queries, "seq").astype(jnp.float32),
        lax.psum(picked_keys, "seq").astype(jnp.float32),
        lax.psum(picked_values, "seq").astype(jnp.float32),
    )
    summary_queries = gathered[0].astype(jnp.bfloat16)
    summary_keys = gathered[1].astype(jnp.bfloat16)
    summary_values = gathered[2].astype(jnp.bfloat16)
    paired = jnp.stack([keys, values], axis=1)
    padded = extended(paired, (("seq", 0),), BLOCK)
    summary_blocks = summary_positions // BLOCK
    offsets = jnp.arange(3, dtype=jnp.int32) - 1
    outputs = []
    for block_index in range(blocks_here):
        query_rows = queries[block_index * BLOCK : (block_index + 1) * BLOCK]
        window = padded[block_index * BLOCK : block_index * BLOCK + 3 * BLOCK]
        my_block = seq_rank * blocks_here + block_index
        neighbour = my_block + offsets
        exists = (neighbour >= 0) & (neighbour < total_blocks)
        band_live = (band_mask[block_index] == 1) & exists
        relative = summary_blocks - my_block
        hits = (relative[:, None] == offsets[None, :]) & band_live[None, :]
        global_live = jnp.logical_not(jnp.any(hits, axis=1))
        outputs.append(
            band_block(
                query_rows,
                window[:, 0],
                window[:, 1],
                band_live,
                summary_keys,
                summary_values,
                global_live,
                scale,
            )
        )
    attended = jnp.concatenate(outputs, axis=0)
    key_heads = keys.reshape(tok_rows, heads_here, HEAD_DIM)
    value_heads = values.reshape(tok_rows, heads_here, HEAD_DIM)
    query_heads = summary_queries.reshape(globals_all, heads_here, HEAD_DIM)
    summary_scores = (
        jnp.einsum("ghd,khd->hgk", query_heads, key_heads, preferred_element_type=jnp.float32)
        * scale
    )
    local_peak = jnp.max(summary_scores, axis=-1)
    summary_peak = lax.pmax(local_peak, "seq")
    summary_weights = jnp.exp(summary_scores - summary_peak[:, :, None])
    part_totals = jnp.transpose(jnp.sum(summary_weights, axis=-1))
    summary_probs = summary_weights.astype(jnp.bfloat16)
    part_sums = jnp.einsum(
        "hgk,khd->ghd", summary_probs, value_heads, preferred_element_type=jnp.float32
    ).reshape(globals_all, width)
    every_sums, every_totals = lax.psum((part_sums, part_totals), "seq")
    own_sums = lax.dynamic_slice_in_dim(every_sums, seq_rank * glob_rows, glob_rows, 0)
    own_totals = lax.dynamic_slice_in_dim(every_totals, seq_rank * glob_rows, glob_rows, 0)
    summary_attended = (
        (own_sums.reshape(glob_rows, heads_here, HEAD_DIM) / own_totals[:, :, None])
        .reshape(glob_rows, width)
        .astype(jnp.bfloat16)
    )
    all_rows = jnp.concatenate([attended, summary_attended], axis=0)
    features = jnp.transpose(
        lax.psum_scatter(
            lax.dot_general(
                out_weight, all_rows, (((0,), (1,)), ((), ())), preferred_element_type=jnp.float32
            ),
            "head",
            scatter_dimension=0,
            tiled=True,
        )
    )
    result = features.astype(jnp.bfloat16)
    return (result[:tok_rows], result[tok_rows:])


def solution(mesh):
    in_specs = (
        P("seq", "head"),
        P("seq", "head"),
        P("seq", "head"),
        P("head", None),
        P("seq", None),
        P(),
    )
    out_specs = (P("seq", "head"), P("seq", "head"))
    return jax.shard_map(
        per_device, mesh=mesh, in_specs=in_specs, out_specs=out_specs, check_vma=False
    )
```

profile of v0, /device:TPU:1, one launch (start us, length us, event | category | flops | bytes accessed | tf_op | source)
XLA Modules:
  0.0 694.0 jit_solution(13615116221969963571)
XLA Ops:
  7.2 2.2 copy.46
  9.4 2.1 copy.45
  11.5 2.2 fusion.59
  13.8 6.5 collective-permute-start
  21.6 4.9 gather_fusion
  26.5 4.9 gather_fusion.1
  31.5 4.9 gather_fusion.2
  36.4 2.9 select_select_fusion.1
  39.3 2.0 copy.41
  41.3 2.0 copy.42
  43.4 2.1 copy.57
  45.4 2.1 copy.58
  47.5 2.1 copy.40
  52.2 2.1 maximum_maximum_fusion
  54.3 1.3 fusion.77
  55.7 3.5 bitcast_reduce_fusion.1
  59.1 3.6 bitcast_reduce_fusion
  62.7 145.0 %all-reduce.6.cloned.1.call-done = (bf16[1024,2,128]{2,0,1:T(8,128)(2,1)}, bf16[1024,2,128]{0,2,1:T(8,128)(2,1)}, bf16[1024,2,128]{2,0,1:T(8,128)(2,1)}) async-done(((bf16[1024,2,128]{2,0,1:T(8,128)(2,1)}, bf16[1024,2,128]{0,2,1:T(8,128)(2,1)}, bf16[1024,2,128]{2,0,1:T(8,128)(2,1)}), (bf16[1024,2,128]{2,0,1:T(8,128)(2,1)}, bf16[1024,2,128]{0,2,1:T(8,128)(2,1)}, ...) | async-done | bytes 1572880 | tf_op jit(solution)/shard_map/psum | solution.py:86
  207.7 1.7 bitcast_reduce_fusion.3
  210.4 3.7 fusion.4
  214.2 2.0 fusion.26
  217.9 1.8 fusion.6
  219.7 4.5 multiply_reduce_fusion
  224.2 33.7 %pmax.7 = f32[2,1024]{1,0:T(2,128)S(1)} all-reduce(f32[2,1024]{1,0:T(2,128)S(1)} %get-tuple-element.30), channel_id=1, replica_groups=mesh['seq'=16,'head'=16] {'seq'}, use_global_device_ids=true, to_apply=%region_14.16 | all-reduce | flops 2048 | bytes 16384 | tf_op jit(solution)/shard_map/pmax | solution.py:129
  257.9 4.8 fusion
  262.7 30.4 %psum.39 = f32[1024,2]{0,1:T(2,128)S(1)} all-reduce(f32[1024,2]{0,1:T(2,128)S(1)} %bitcast.151), channel_id=1, replica_groups=mesh['seq'=16,'head'=16] {'seq'}, use_global_device_ids=true, to_apply=%region_17.19 | all-reduce | flops 2048 | bytes 16384 | tf_op jit(solution)/shard_map/psum | solution.py:136
  293.1 6.1 fusion.8
  299.4 4.5 fusion.51
  305.2 4.3 fusion.45
  309.6 163.5 %all-reduce.4.cloned.1.call-done = f32[1024,256]{0,1:T(8,128)} async-done(((f32[1024,256]{0,1:T(8,128)}), f32[1024,256]{0,1:T(8,128)}) %all-reduce.4.cloned.1.call-update) | async-done | bytes 1048592 | tf_op jit(solution)/shard_map/psum | solution.py:136
  474.1 8.6 %convolution_bitcast_fusion = f32[4096,1088]{0,1:T(8,128)} fusion(bf16[256,4096]{1,0:T(8,128)(2,1)S(1)} %copy-done, bf16[64,256]{0,1:T(8,128)(2,1)S(1)} %fusion.63, bf16[512,256]{0,1:T(8,128)(2,1)S(1)} %bitcast.150, bf16[512,256]{0,1:T(8,128)(2,1)S(1)} %bitcast.149), kind=kOutput, calls=%fused_computation.3 | convolution fusion | flops 2283372544 | bytes 20480000 | tf_op jit(solution)/shard_map/dot_general | solution.py:147
  482.7 202.0 %reduce-scatter.2.cloned.1.call-done = f32[256,1088]{0,1:T(8,128)} async-done(((f32[4096,1088]{0,1:T(8,128)}), f32[256,1088]{0,1:T(8,128)}) %reduce-scatter.2.cloned.1.call-update) | async-done | bytes 1114128 | tf_op jit(solution)/shard_map/reduce_scatter | solution.py:146
  (72 shorter events, 11.7 us)
Async XLA Ops:
  7.2 466.9 %copy-start = (bf16[256,4096]{1,0:T(8,128)(2,1)S(1)}, bf16[256,4096]{1,0:T(8,128)(2,1)}, u32[]{:S(2)}) copy-start(bf16[256,4096]{1,0:T(8,128)(2,1)} %param.11) | copy-start | bytes 6291460
  7.2 14.4 %copy-start.2 = (bf16[1024,256]{1,0:T(8,128)(2,1)S(1)}, bf16[1024,256]{1,0:T(8,128)(2,1)}, u32[]{:S(2)}) copy-start(bf16[1024,256]{1,0:T(8,128)(2,1)} %param.10) | copy-start | bytes 1572868
  7.2 14.3 %copy-start.11 = (s32[1024]{0:T(1024)S(1)}, s32[1024]{0:T(1024)}, u32[]{:S(2)}) copy-start(s32[1024]{0:T(1024)} %param.13) | copy-start | bytes 12292
  7.2 200.5 %all-reduce.6.cloned.1.call-start = ((), (), s32[]{:S(2)}) async-start(), calls=%async_computation.3 | async-start | bytes 3145728 | tf_op jit(solution)/shard_map/psum | solution.py:86
  9.4 17.1 %copy-start.1 = (bf16[1024,256]{1,0:T(8,128)(2,1)S(1)}, bf16[1024,256]{1,0:T(8,128)(2,1)}, u32[]{:S(2)}) copy-start(bf16[1024,256]{1,0:T(8,128)(2,1)} %param.9) | copy-start | bytes 1572868
  13.8 38.4 %collective-permute-start = (bf16[512,2,256]{0,2,1:T(8,128)(2,1)}, bf16[512,2,256]{0,2,1:T(8,128)(2,1)}, u32[]{:S(2)}, u32[]{:S(2)}) collective-permute-start(bf16[512,2,256]{0,2,1:T(8,128)(2,1)} %get-tuple-element.14), channel_id=1, source_target_pairs={{0,16},{16,32},{32,48},{48,64},{64,80},{80,96},{96,112},{112,128},... | collective-permute-start | bytes 1572872 | tf_op jit(solution)/shard_map/ppermute | solution.py:20
  20.2 32.0 %collective-permute-start.1 = (bf16[512,2,256]{0,2,1:T(8,128)(2,1)}, bf16[512,2,256]{0,2,1:T(8,128)(2,1)}, u32[]{:S(2)}, u32[]{:S(2)}) collective-permute-start(bf16[512,2,256]{0,2,1:T(8,128)(2,1)} %get-tuple-element.15), channel_id=1, source_target_pairs={{16,0},{32,16},{48,32},{64,48},{80,64},{96,80},{112,96},{128,112},... | collective-permute-start | bytes 1572872 | tf_op jit(solution)/shard_map/ppermute | solution.py:22
  26.5 5.0 copy-start.3
  39.3 10.6 %copy-start.12 = (s32[2,3]{1,0:T(2,128)S(1)}, s32[2,3]{1,0:T(2,128)}, u32[]{:S(2)}) copy-start(s32[2,3]{1,0:T(2,128)} %param.12) | copy-start | bytes 76
  49.6 423.4 %all-reduce.4.cloned.1.call-start = ((), (), s32[]{:S(2)}) async-start(), calls=%async_computation.1 | async-start | bytes 2097152 | tf_op jit(solution)/shard_map/psum | solution.py:136
  210.4 3.8 copy-start.13
  214.1 2.0 copy-start.7
  214.1 3.7 slice-start
  216.1 1.7 slice-start.1
  216.9 2.8 copy-start.4
  217.8 1.9 copy-start.10
  257.9 35.2 %copy-start.6 = (bf16[1024,256]{0,1:T(8,128)(2,1)S(1)}, bf16[1024,256]{0,1:T(8,128)(2,1)}, u32[]{:S(2)}) copy-start(bf16[1024,256]{0,1:T(8,128)(2,1)} %copy.46) | copy-start | bytes 1572868
  293.1 6.2 copy-start.9
  299.3 385.4 %reduce-scatter.2.cloned.1.call-start = ((), (), s32[]{:S(2)}) async-start(), calls=%async_computation.2 | async-start | bytes 18939904 | tf_op jit(solution)/shard_map/reduce_scatter | solution.py:146
  299.4 4.7 copy-start.5
  299.4 4.6 copy-start.14
  303.9 1.3 copy-start.8
Sparse Core Ops, SparseCore 0:
  49.7 157.8 all-reduce.5
  299.4 173.5 all-reduce.3
  482.9 201.8 reduce-scatter.1
where the time goes:
time: 695 us; the launch traced here: 694 us
  waiting for transfers between devices  511 us (74%)
  blocking collectives  64.1 us (9%)
  matrix products  40.8 us (6%)
  local copies, waits for them, and re-layouts  34.6 us (5%)
  other arithmetic  21.9 us (3%)
  between operations  14.1 us (2%)
  starting transfers between devices  8.04 us (1%)
    reduce_scatter x1, waiting for transfers between devices, per_device(): lax.psum_scatter(lax.dot_general(out_weight, all_rows, (((0,), (1,)), (()...  202 us
    psum x1, waiting for transfers between devices, per_device(): every_sums, every_totals = lax.psum((part_sums, part_totals), 'seq')  163 us
    psum x1, waiting for transfers between devices, per_device(): lax.psum(picked_queries, 'seq').astype(jnp.float32)  145 us
    pmax x1, blocking collectives, per_device(): summary_peak = lax.pmax(local_peak, 'seq')  33.7 us
    psum x1, blocking collectives, per_device(): every_sums, every_totals = lax.psum((part_sums, part_totals), 'seq')  30.4 us
  transfers between devices with their start and end apart: 5, of which 3 were waited for; matrix products, arithmetic and copies ran while one was open for 7% of the time, Pallas kernels for 0%

commit v1 on v0

--- a/solution.py
+++ b/solution.py
@@ -1,12 +1,41 @@
+import functools
 import math
 
 import jax
 import jax.numpy as jnp
 from jax import lax
+from jax.experimental import pallas as pl
+from jax.experimental.pallas import tpu as pltpu
 from jax.sharding import PartitionSpec as P
 
 HEAD_DIM = 128
 BLOCK = 512
+NEG = -1e30
+F32 = jnp.float32
+BF16 = jnp.bfloat16
+VMEM = pl.BlockSpec(memory_space=pltpu.VMEM)
+SMEM = pl.BlockSpec(memory_space=pltpu.SMEM)
+PARAMS = pltpu.CompilerParams(vmem_limit_bytes=50 * 1024 * 1024)
+
+
+def kernel_call(body, outs, ins, scratch=(), smem=()):
+    specs = [SMEM if i in smem else VMEM for i in range(len(ins))]
+    return pl.pallas_call(
+        body,
+        out_shape=outs,
+        in_specs=specs,
+        out_specs=jax.tree.map(lambda _: VMEM, outs),
+        scratch_shapes=list(scratch),
+        compiler_params=PARAMS,
+    )(*ins)
+
+
+def dot_nt(a, b):
+    return lax.dot_general(a, b, (((1,), (1,)), ((), ())), preferred_element_type=F32)
+
+
+def dot_nn(a, b):
+    return lax.dot_general(a, b, (((1,), (0,)), ((), ())), preferred_element_type=F32)
 
 
 def extended(cells, sides, width):
@@ -65,7 +94,7 @@
     return result.reshape(count, heads_here * HEAD_DIM).astype(jnp.bfloat16)
 
 
-def per_device(queries, keys, values, out_weight, band_mask, summary_positions):
+def general(queries, keys, values, out_weight, band_mask, summary_positions, starts):
     tok_rows, width = queries.shape
     heads_here = width // HEAD_DIM
     blocks_here = tok_rows // BLOCK
@@ -156,6 +185,360 @@
     return (result[:tok_rows], result[tok_rows:])
 
 
+GROUP = 4
+SLOTS = 80
+CODE = 128
+
+
+def pick_body(place, q, k, v, *refs):
+    outs, first_kv, last_kv = refs[:GROUP], refs[GROUP], refs[GROUP + 1]
+    rows = q.shape[0]
+    width = q.shape[1]
+    lanes = lax.broadcasted_iota(jnp.int32, (SLOTS, rows), 1)
+    for d in range(GROUP):
+        hot = jnp.where(place[d * SLOTS : (d + 1) * SLOTS, :] == lanes, 1.0, 0.0).astype(BF16)
+        outs[d][:, :width] = dot_nn(hot, q[...]).astype(BF16)
+        outs[d][:, width : 2 * width] = dot_nn(hot, k[...]).astype(BF16)
+        outs[d][:, 2 * width :] = dot_nn(hot, v[...]).astype(BF16)
+    first_kv[:, :width] = k[:BLOCK, :]
+    first_kv[:, width:] = v[:BLOCK, :]
+    last_kv[:, :width] = k[rows - BLOCK :, :]
+    last_kv[:, width:] = v[rows - BLOCK :, :]
+
+
+def band_body(factor, live, q, k, v, before, after, acc, stat, ke, ve):
+    rows, width = q.shape
+    heads = width // HEAD_DIM
+    tile = 256
+    window = 3 * BLOCK
+    ke[:BLOCK, :] = before[:, :width]
+    ke[BLOCK : BLOCK + rows, :] = k[...]
+    ke[BLOCK + rows :, :] = after[:, :width]
+    for h in range(heads):
+        src = slice(h * HEAD_DIM, (h + 1) * HEAD_DIM)
+        off = slice(width + h * HEAD_DIM, width + (h + 1) * HEAD_DIM)
+        dst = slice(2 * h * HEAD_DIM, (2 * h + 1) * HEAD_DIM)
+        one = slice((2 * h + 1) * HEAD_DIM, (2 * h + 2) * HEAD_DIM)
+        ve[:BLOCK, dst] = before[:, off]
+        ve[BLOCK : BLOCK + rows, dst] = v[:, src]
+        ve[BLOCK + rows :, dst] = after[:, off]
+        ve[:, one] = jnp.ones((ve.shape[0], HEAD_DIM), BF16)
+
+    def step(t, carry):
+        block = t // (BLOCK // tile)
+        at = pl.multiple_of(t * tile, tile)
+        base = pl.multiple_of(block * BLOCK, BLOCK)
+        for h in range(heads):
+            cols = slice(h * HEAD_DIM, (h + 1) * HEAD_DIM)
+            qt = q[pl.ds(at, tile), cols]
+            parts = []
+            for j in range(3):
+                s = dot_nt(qt, ke[pl.ds(base + j * BLOCK, BLOCK), cols]) * factor
+                parts.append(jnp.where(live[block, j] == 1, s, NEG))
+            peak = functools.reduce(jnp.maximum, [jnp.max(s, axis=1, keepdims=True) for s in parts])
+            both = None
+            for j in range(3):
+                p = jnp.exp2(parts[j] - peak).astype(BF16)
+                o = dot_nn(
+                    p, ve[pl.ds(base + j * BLOCK, BLOCK), 2 * h * HEAD_DIM : (2 * h + 2) * HEAD_DIM]
+                )
+                both = o if both is None else both + o
+            acc[pl.ds(at, tile), cols] = both[:, :HEAD_DIM]
+            stat[pl.ds(at, tile), 2 * h * HEAD_DIM : (2 * h + 1) * HEAD_DIM] = both[:, HEAD_DIM:]
+            stat[pl.ds(at, tile), (2 * h + 1) * HEAD_DIM : (2 * h + 2) * HEAD_DIM] = (
+                jnp.broadcast_to(peak, (tile, HEAD_DIM))
+            )
+        return carry
+
+    lax.fori_loop(0, rows // tile, step, 0)
+
+
+def main_body(factor, pieces, places, q, bias, acc, stat, *refs):
+    ins, (out, qg), (wide, kg, vg) = refs[:pieces], refs[pieces : pieces + 2], refs[pieces + 2 :]
+    rows, width = q.shape
+    heads = width // HEAD_DIM
+    total = kg.shape[0]
+    tile = 256
+    wide[...] = jnp.zeros(wide.shape, F32)
+    n = 0
+    for ref in ins:
+        for b in range(ref.shape[0] // SLOTS):
+            at = places[n]
+            n += 1
+            block = ref[b * SLOTS : (b + 1) * SLOTS, :].astype(F32)
+            block = jnp.concatenate([block, jnp.zeros((8, block.shape[1]), F32)], axis=0)
+            block = pltpu.roll(block, at % 8, 0)
+            wide[pl.ds(pl.multiple_of(at // 8 * 8, 8), SLOTS + 8), :] += block
+    qg[...] = wide[:total, :width].astype(BF16)
+    kg[...] = wide[:total, width : 2 * width].astype(BF16)
+    for h in range(heads):
+        vg[:, 2 * h * HEAD_DIM : (2 * h + 1) * HEAD_DIM] = wide[
+            :total, 2 * width + h * HEAD_DIM : 2 * width + (h + 1) * HEAD_DIM
+        ].astype(BF16)
+        vg[:, (2 * h + 1) * HEAD_DIM : (2 * h + 2) * HEAD_DIM] = jnp.ones((total, HEAD_DIM), BF16)
+
+    def step(t, carry):
+        block = t // (BLOCK // tile)
+        at = pl.multiple_of(t * tile, tile)
+        for h in range(heads):
+            cols = slice(h * HEAD_DIM, (h + 1) * HEAD_DIM)
+            s = dot_nt(q[pl.ds(at, tile), cols], kg[:, cols]) * factor
+            s = s + bias[block]
+            band_sum = stat[pl.ds(at, tile), 2 * h * HEAD_DIM : (2 * h + 1) * HEAD_DIM]
+            band_peak = stat[pl.ds(at, tile), (2 * h + 1) * HEAD_DIM : (2 * h + 2) * HEAD_DIM]
+            peak = jnp.maximum(jnp.max(s, axis=1, keepdims=True), band_peak[:, :1])
+            p = jnp.exp2(s - peak).astype(BF16)
+            o = dot_nn(p, vg[:, 2 * h * HEAD_DIM : (2 * h + 2) * HEAD_DIM])
+            back = jnp.exp2(band_peak - peak)
+            num = o[:, :HEAD_DIM] + back * acc[pl.ds(at, tile), cols]
+            den = o[:, HEAD_DIM:] + back * band_sum
+            out[pl.ds(at, tile), cols] = (num / den).astype(BF16)
+        return carry
+
+    lax.fori_loop(0, rows // tile, step, 0)
+
+
+def summary_body(factor, qg, k, v, out, ve):
+    rows, width = qg.shape
+    heads = width // HEAD_DIM
+    tile = 256
+    for h in range(heads):
+        ve[:, 2 * h * HEAD_DIM : (2 * h + 1) * HEAD_DIM] = v[:, h * HEAD_DIM : (h + 1) * HEAD_DIM]
+        ve[:, (2 * h + 1) * HEAD_DIM : (2 * h + 2) * HEAD_DIM] = jnp.ones(
+            (ve.shape[0], HEAD_DIM), BF16
+        )
+    lane = lax.broadcasted_iota(jnp.int32, (tile, CODE), 1)
+
+    def step(t, carry):
+        at = pl.multiple_of(t * tile, tile)
+        code = jnp.zeros((tile, CODE), F32)
+        for h in range(heads):
+            cols = slice(h * HEAD_DIM, (h + 1) * HEAD_DIM)
+            s = dot_nt(qg[pl.ds(at, tile), cols], k[:, cols]) * factor
+            peak = jnp.max(s, axis=1, keepdims=True)
+            p = jnp.exp2(s - peak).astype(BF16)
+            o = dot_nn(p, ve[:, 2 * h * HEAD_DIM : (2 * h + 2) * HEAD_DIM])
+            den = o[:, HEAD_DIM:]
+            out[pl.ds(at, tile), cols] = (o[:, :HEAD_DIM] / den).astype(BF16)
+            size = peak + jnp.log2(den)
+            for piece in range(3):
+                part = size.astype(BF16).astype(F32)
+                code = jnp.where(lane == 3 * h + piece, part, code)
+                size = size - part
+        out[pl.ds(at, tile), width:] = code.astype(BF16)
+        return carry
+
+    lax.fori_loop(0, rows // tile, step, 0)
+
+
+def merge_body(sent, out):
+    count, rows, full = sent.shape
+    width = full - CODE
+    for h in range(width // HEAD_DIM):
+        cols = slice(h * HEAD_DIM, (h + 1) * HEAD_DIM)
+        sizes = []
+        for s in range(count):
+            code = sent[s, :, width:].astype(F32)
+            sizes.append(
+                code[:, 3 * h : 3 * h + 1]
+                + code[:, 3 * h + 1 : 3 * h + 2]
+                + code[:, 3 * h + 2 : 3 * h + 3]
+            )
+        peak = functools.reduce(jnp.maximum, sizes)
+        num = jnp.zeros((rows, HEAD_DIM), F32)
+        den = jnp.zeros((rows, 1), F32)
+        for s in range(count):
+            w = jnp.exp2(sizes[s] - peak)
+            num = num + w * sent[s, :, cols].astype(F32)
+            den = den + w
+        out[:, cols] = (num / den).astype(BF16)
+
+
+def project_body(layout, weights_count, side, *refs):
+    pieces = len(layout)
+    ins, weights = refs[:pieces], refs[pieces : pieces + weights_count]
+    mine, other = refs[pieces + weights_count :]
+    width = mine.shape[1]
+    me = side[0]
+    bands = {}
+    for i, (first, count, w) in enumerate(layout):
+        bands.setdefault((first, count), [])
+    edges = sorted({f for f, c, w in layout} | {f + c for f, c, w in layout})
+    for out, who in ((mine, me), (other, 1 - me)):
+        cols = pl.ds(pl.multiple_of(who * width, width), width)
+        for low, high in zip(edges[:-1], edges[1:]):
+            total = None
+            for i, (first, count, w) in enumerate(layout):
+                if first <= low and high <= first + count:
+                    part = dot_nn(ins[i][low - first : high - first, :], weights[w][:, cols])
+                    total = part if total is None else total + part
+            out[low:high, :] = total
+
+
+def balanced(queries, keys, values, out_weight, band_mask, positions, starts):
+    rows, width = queries.shape
+    seq_count = lax.axis_size("seq")
+    head_count = lax.axis_size("head")
+    rank = lax.axis_index("seq")
+    place = lax.axis_index("head")
+    blocks = rows // BLOCK
+    total = positions.shape[0]
+    home_rows = total // seq_count
+    first = rank * rows
+    factor = (1.0 / math.sqrt(HEAD_DIM)) * math.log2(math.e)
+    shape = jax.ShapeDtypeStruct
+
+    def seq_pp(x, f):
+        return lax.ppermute(x, "seq", [(i, f(i) % seq_count) for i in range(seq_count)])
+
+    def head_pp(x, f):
+        return lax.ppermute(x, "head", [(i, f(i) % head_count) for i in range(head_count)])
+
+    group, member = rank // GROUP, rank % GROUP
+    begin = starts[group]
+    count = starts[group + 1] - begin
+    order = member ^ jnp.arange(GROUP, dtype=jnp.int32)
+    slot = (order[:, None] * SLOTS + jnp.arange(SLOTS, dtype=jnp.int32)[None, :]).reshape(-1)
+    padded = jnp.concatenate([positions, jnp.zeros((GROUP * SLOTS,), jnp.int32)])
+    wanted = jnp.where(slot < count, jnp.take(padded, begin + slot) - first, -1)[:, None]
+    pick = shape((SLOTS, 3 * width), BF16)
+    edge = shape((BLOCK, 2 * width), BF16)
+    *picked, first_kv, last_kv = kernel_call(
+        pick_body, [pick] * GROUP + [edge, edge], [wanted, queries, keys, values]
+    )
+    home = picked[0]
+    for d in range(1, GROUP):
+        home = home + seq_pp(picked[d], lambda i: i ^ d)
+    pair = jnp.concatenate([home, seq_pp(home, lambda i: i ^ 1)], axis=0)
+    up = lambda x: seq_pp(x, lambda i: i + 2)
+    down = lambda x: seq_pp(x, lambda i: i - 2)
+    a1, b1 = up(pair), down(pair)
+    a2, b2 = up(a1), down(b1)
+    a3, b3 = up(a2), down(b2)
+    a4, b4 = up(a3[:SLOTS]), down(b3[SLOTS:])
+    pieces = [pair, a1, b1, a2, b2, a3, b3, a4, b4]
+    steps = [0, -1, 1, -2, 2, -3, 3, -4]
+    owners = []
+    for d in steps:
+        owners += [rank + 2 * d, (rank ^ 1) + 2 * d]
+    owners = jnp.stack(owners) % seq_count
+    places = jnp.take(starts, owners // GROUP) + SLOTS * (owners % GROUP)
+
+    before = seq_pp(last_kv, lambda i: i + 1)
+    after = seq_pp(first_kv, lambda i: i - 1)
+    offsets = jnp.arange(3, dtype=jnp.int32) - 1
+    my_block = rank * blocks + jnp.arange(blocks, dtype=jnp.int32)
+    neighbour = my_block[:, None] + offsets[None, :]
+    live = (band_mask == 1) & (neighbour >= 0) & (neighbour < seq_count * blocks)
+    relative = (positions // BLOCK)[None, :] - my_block[:, None]
+    hits = (relative[:, None, :] == offsets[None, :, None]) & live[:, :, None]
+    bias = jnp.where(jnp.any(hits, axis=1), jnp.float32(NEG), jnp.float32(0.0))[:, None, :]
+    acc, stat = kernel_call(
+        functools.partial(band_body, factor),
+        [shape((rows, width), F32), shape((rows, 2 * width), F32)],
+        [live.astype(jnp.int32), queries, keys, values, before, after],
+        [pltpu.VMEM((rows + 2 * BLOCK, width), BF16), pltpu.VMEM((rows + 2 * BLOCK, 2 * width), BF16)],
+        smem=(0,),
+    )
+
+    chips = head_count // 2
+    chip, core = place // 2, place % 2
+    cx, cy = chip // 2, chip % 2
+    by_chip = out_weight.reshape(width, chips, 2 * width)
+
+    def weight_from(dx, dy):
+        to = ((cx + dx) % 4) * 2 + (cy ^ dy)
+        part = lax.dynamic_index_in_dim(by_chip, to, axis=1, keepdims=False)
+        if dx == 0 and dy == 0:
+            return part
+        return head_pp(part, lambda i: ((i + 4 * dx) % 16) ^ (2 * dy))
+
+    weights = [weight_from(dx, dy) for dy in range(2) for dx in range(4)]
+
+    attended, summary_queries = kernel_call(
+        functools.partial(main_body, factor, len(pieces)),
+        [shape((rows, width), BF16), shape((total, width), BF16)],
+        [places, queries, bias, acc, stat] + pieces,
+        [
+            pltpu.VMEM((total + GROUP * SLOTS + 8, 3 * width), F32),
+            pltpu.VMEM((total, width), BF16),
+            pltpu.VMEM((total, 2 * width), BF16),
+        ],
+        smem=(0,),
+    )
+
+    xu = lambda x: head_pp(x, lambda i: i + 4)
+    xd = lambda x: head_pp(x, lambda i: i - 4)
+    yy = lambda x: head_pp(x, lambda i: i ^ 2)
+    half = rows // 2
+    layout, parts = [], []
+
+    def around(block, dy):
+        u1, d1 = xu(block), xd(block)
+        u2, d2 = xu(u1[:half]), xd(d1[half:])
+        for piece, at, size, dx in (
+            (block, 0, rows, 0),
+            (u1, 0, rows, 1),
+            (d1, 0, rows, 3),
+            (u2, 0, half, 2),
+            (d2, half, half, 2),
+        ):
+            parts.append(piece)
+            layout.append((at, size, 4 * dy + dx))
+
+    across = yy(attended)
+    around(attended, 0)
+    around(across, 1)
+
+    partial = kernel_call(
+        functools.partial(summary_body, factor),
+        shape((total, width + CODE), BF16),
+        [summary_queries, keys, values],
+        [pltpu.VMEM((rows, 2 * width), BF16)],
+    )
+    sent = lax.all_to_all(
+        partial.reshape(seq_count, home_rows, width + CODE), "seq", 0, 0, tiled=True
+    )
+    own = kernel_call(merge_body, shape((home_rows, width), BF16), [sent])
+    own_across = yy(own)
+    for block, dy in ((own, 0), (own_across, 1)):
+        for dx in range(4):
+            parts.append(block if dx == 0 else head_pp(block, lambda i: i + 4 * dx))
+            layout.append((rows, home_rows, 4 * dy + dx))
+
+    full = shape((rows + home_rows, width), F32)
+    mine, other = kernel_call(
+        lambda *refs: project_body(layout, len(weights), refs[0], *refs[1:]),
+        [full, full],
+        [core[None].astype(jnp.int32)] + parts + weights,
+        smem=(0,),
+    )
+    result = (mine + head_pp(other, lambda i: i ^ 1)).astype(BF16)
+    return (result[:rows], result[rows:])
+
+
+def per_device(queries, keys, values, out_weight, band_mask, summary_positions):
+    rows = queries.shape[0]
+    seq_count = lax.axis_size("seq")
+    edges = jnp.arange(seq_count // GROUP + 1, dtype=jnp.int32) * (GROUP * rows)
+    starts = jnp.sum(
+        (summary_positions[None, :] < edges[:, None]).astype(jnp.int32), axis=1, dtype=jnp.int32
+    )
+    fits = jnp.max(starts[1:] - starts[:-1]) <= GROUP * SLOTS
+    return lax.cond(
+        fits,
+        balanced,
+        general,
+        queries,
+        keys,
+        values,
+        out_weight,
+        band_mask,
+        summary_positions,
+        starts,
+    )
+
+
 def solution(mesh):
     in_specs = (
         P("seq", "head"),

time: 695 us -> 227 us (0.33)
  waiting for transfers between devices: 511 us -> 77.6 us
  blocking collectives: 64.1 us -> 0 us
  starting transfers between devices: 8.04 us -> 59 us
  matrix products: 40.8 us -> 0 us
  Pallas kernels: 0 us -> 34.6 us
  other arithmetic: 21.9 us -> 5.21 us
  local copies, waits for them, and re-layouts: 34.6 us -> 20.7 us
  loops' own time: 0 us -> 10.8 us
    psum x2 -> x0, waiting for transfers between devices: 308 us -> none  [the longest x1 163 us: per_device(): every_sums, every_totals = lax.psum((part_sums, part_totals), 'seq')]
    reduce_scatter x1 -> x0, waiting for transfers between devices: 202 us -> none  [per_device(): lax.psum_scatter(lax.dot_general(out_weight, all_rows, (((0,), (1,)), (()...]
    ppermute x2 -> x38, waiting for transfers between devices: 0.01 us -> 77.6 us  [the longest x24 39.7 us: head_pp(): lax.ppermute(x, 'head', [(i, f(i) % head_count) for i in range(head_count)])]
    ppermute x2 -> x38, starting transfers between devices: 7.74 us -> 54.4 us  [the longest x24 27.4 us: head_pp(): lax.ppermute(x, 'head', [(i, f(i) % head_count) for i in range(head_count)])]
    dot_general x11 -> x0, matrix products: 40.8 us -> none  [the longest x2 8.83 us: band_block(): jnp.einsum('hqk,khd->qhd', band_probs, value_heads, preferred_element_typ...]
    pallas_call x0 -> x6, Pallas kernels: none -> 34.6 us  [kernel_call(): pl.pallas_call(body, out_shape=outs, in_specs=specs, out_specs=jax.tree.m...]
    pmax x1 -> x0, blocking collectives: 33.7 us -> none  [per_device(): summary_peak = lax.pmax(local_peak, 'seq')]
    psum x1 -> x0, blocking collectives: 30.4 us -> none  [per_device(): every_sums, every_totals = lax.psum((part_sums, part_totals), 'seq')]
  transfers between devices with their start and end apart: 5 -> 39, of which waited for: 3 -> 14; matrix products, arithmetic and copies ran while one was open for 7% -> 6% of each run, Pallas kernels for 0% -> 5%
where the time goes in v1:
time: 227 us; the launch traced here: 223 us
  waiting for transfers between devices  77.6 us (34%)
  starting transfers between devices  59 us (26%)
  Pallas kernels  34.6 us (15%)
  local copies, waits for them, and re-layouts  20.7 us (9%)
  between operations  14.9 us (7%)
  loops' own time  10.8 us (5%)
  other arithmetic  5.21 us (2%)
    ppermute x24, waiting for transfers between devices, head_pp(): lax.ppermute(x, 'head', [(i, f(i) % head_count) for i in range(head_count)])  39.7 us
    ppermute x14, waiting for transfers between devices, seq_pp(): lax.ppermute(x, 'seq', [(i, f(i) % seq_count) for i in range(seq_count)])  37.9 us
    pallas_call x6, Pallas kernels, kernel_call(): pl.pallas_call(body, out_shape=outs, in_specs=specs, out_specs=jax.tree.m...  34.6 us
    ppermute x24, starting transfers between devices, head_pp(): lax.ppermute(x, 'head', [(i, f(i) % head_count) for i in range(head_count)])  27.4 us
    ppermute x14, starting transfers between devices, seq_pp(): lax.ppermute(x, 'seq', [(i, f(i) % seq_count) for i in range(seq_count)])  27 us
    another operation x1, loops' own time, per_device(): lax.cond(fits, balanced, general, queries, keys, values, out_weight, band...  10.8 us
    dynamic_slice x1, local copies, waits for them, and re-layouts, weight_from(): part = lax.dynamic_index_in_dim(by_chip, to, axis=1, keepdims=False)  5.05 us
    all_to_all x1, starting transfers between devices, balanced(): lax.all_to_all(partial.reshape(seq_count, home_rows, width + CODE), 'seq'...  4.67 us
  transfers between devices with their start and end apart: 39, of which 14 were waited for; matrix products, arithmetic and copies ran while one was open for 6% of the time, Pallas kernels for 5%

profile of v1, /device:TPU:1, one launch (start us, length us, event | category | flops | bytes accessed | tf_op | source)
XLA Modules:
  0.0 222.9 jit_solution(12101066760340460007)
XLA Ops:
  9.4 203.1 %conditional.1 = (bf16[1088,256]{1,0:T(8,128)(2,1)}) conditional(s32[]{:T(128)} %convert_element_type.59, (s32[1024]{0:T(1024)}, bf16[1024,256]{1,0:T(8,128)(2,1)}, s32[2,3]{1,0:T(2,128)}, bf16[1024,256]{1,0:T(8,128)(2,1)}, bf16[1024,256]{1,0:T(8,128)(2,1)}, /*index=5*/bf16[256,4096]{1,0:T(8,128)(2,1)}) %tuple.16, (s32[5]{0:T(128)S(1)}, ...), branch_computations={%region_2.23_spmd, %region_22.25_spmd} | conditional | flops 6131220480 | bytes 322621952 | solution.py:528
  22.1 2.2 %gather_fusion.1 = s32[320]{0:T(512)S(1)} fusion(s32[1344]{0:T(1024)S(1)} %concatenate.35, s32[1024]{0:T(1024)S(1)} %pad_clamp_fusion), kind=kCustom, calls=%fused_computation.2 | custom fusion | bytes 3840 | tf_op jit(solution)/shard_map/cond/branch_1_fun/jit(_take)/gather | solution.py:403
  24.5 3.3 %branch_1_fun.6 = (bf16[80,768]{1,0:T(8,128)(2,1)S(1)}, bf16[80,768]{1,0:T(8,128)(2,1)S(1)}, bf16[80,768]{1,0:T(8,128)(2,1)S(1)}, bf16[80,768]{1,0:T(8,128)(2,1)...) custom-call(s32[320,1]{1,0:T(8,128)S(1)} %fusion.78.place, bf16[1024,256]{1,0:T(8,128)(2,1)} %get-tuple-element.34.q, ...), custom_call_target="tpu_custom_call" | custom-call | tf_op jit(solution)/shard_map/cond/branch_1_fun/pallas_call | solution.py:23
  27.8 3.7 %collective-permute-start.2 = (bf16[80,768]{1,0:T(8,128)(2,1)S(1)}, bf16[80,768]{1,0:T(8,128)(2,1)S(1)}, u32[]{:S(2)}, u32[]{:S(2)}) collective-permute-start(bf16[80,768]{1,0:T(8,128)(2,1)S(1)} %get-tuple-element.44), channel_id=1, source_target_pairs={{0,16},{16,0},{32,48},{48,32},{64,80},{80,64},{96,112},{112,96},{1... | collective-permute-start | bytes 368648 | tf_op jit(solution)/shard_map/cond/branch_1_fun/ppermute | solution.py:392
  33.2 2.7 %collective-permute-start = (bf16[512,512]{1,0:T(8,128)(2,1)}, bf16[512,512]{1,0:T(8,128)(2,1)S(1)}, u32[]{:S(2)}, u32[]{:S(2)}) collective-permute-start(bf16[512,512]{1,0:T(8,128)(2,1)} %get-tuple-element.39), channel_id=1, source_target_pairs={{0,16},{16,32},{32,48},{48,64},{64,80},{80,96},{96,112},{112,128},... | collective-permute-start | bytes 1572872 | tf_op jit(solution)/shard_map/cond/branch_1_fun/ppermute | solution.py:392
  35.9 5.1 %collective-permute-start.1 = (bf16[512,512]{1,0:T(8,128)(2,1)S(1)}, bf16[512,512]{1,0:T(8,128)(2,1)S(1)}, u32[]{:S(2)}, u32[]{:S(2)}) collective-permute-start(bf16[512,512]{1,0:T(8,128)(2,1)S(1)} %get-tuple-element.40), channel_id=1, source_target_pairs={{0,240},{16,0},{32,16},{48,32},{64,48},{80,64},{96,80},{112,96},{1... | collective-permute-start | bytes 1572872 | tf_op jit(solution)/shard_map/cond/branch_1_fun/ppermute | solution.py:392
  41.3 24.3 %collective-permute-done.5 = bf16[80,768]{1,0:T(8,128)(2,1)S(1)} collective-permute-done((bf16[80,768]{1,0:T(8,128)(2,1)S(1)}, bf16[80,768]{1,0:T(8,128)(2,1)S(1)}, u32[]{:S(2)}, u32[]{:S(2)}) %collective-permute-start.5) | collective-permute-done | bytes 122912 | tf_op jit(solution)/shard_map/cond/branch_1_fun/ppermute | solution.py:392
  66.2 4.6 %collective-permute-start.7 = (bf16[160,768]{1,0:T(8,128)(2,1)S(1)}, bf16[160,768]{1,0:T(8,128)(2,1)S(1)}, u32[]{:S(2)}, u32[]{:S(2)}) collective-permute-start(bf16[160,768]{1,0:T(8,128)(2,1)S(1)} %pad_maximum_fusion.2.refs_0_), channel_id=1, source_target_pairs={{0,224},{16,240},{32,0},{48,16},{64,32},{80,48},{96,64},{112,80},{... | collective-permute-start | bytes 737288 | tf_op jit(solution)/shard_map/cond/branch_1_fun/ppermute | solution.py:392
  71.0 5.6 %collective-permute-done.6.refs_1_ = bf16[160,768]{1,0:T(8,128)(2,1)S(1)} collective-permute-done((bf16[160,768]{1,0:T(8,128)(2,1)S(1)}, bf16[160,768]{1,0:T(8,128)(2,1)S(1)}, u32[]{:S(2)}, u32[]{:S(2)}) %collective-permute-start.6) | collective-permute-done | bytes 245792 | tf_op jit(solution)/shard_map/cond/branch_1_fun/ppermute | solution.py:392
  76.6 2.7 %collective-permute-start.9 = (bf16[160,768]{1,0:T(8,128)(2,1)S(1)}, bf16[160,768]{1,0:T(8,128)(2,1)S(1)}, u32[]{:S(2)}, u32[]{:S(2)}) collective-permute-start(bf16[160,768]{1,0:T(8,128)(2,1)S(1)} %collective-permute-done.7.refs_2_), channel_id=1, source_target_pairs={{0,224},{16,240},{32,0},{48,16},{64,32},{80,48},{96,64},{112,80},{... | collective-permute-start | bytes 737288 | tf_op jit(solution)/shard_map/cond/branch_1_fun/ppermute | solution.py:392
  79.5 4.7 %collective-permute-done.8.refs_3_ = bf16[160,768]{1,0:T(8,128)(2,1)S(1)} collective-permute-done((bf16[160,768]{1,0:T(8,128)(2,1)S(1)}, bf16[160,768]{1,0:T(8,128)(2,1)S(1)}, u32[]{:S(2)}, u32[]{:S(2)}) %collective-permute-start.8) | collective-permute-done | bytes 245792 | tf_op jit(solution)/shard_map/cond/branch_1_fun/ppermute | solution.py:392
  84.3 2.7 %collective-permute-start.11 = (bf16[160,768]{1,0:T(8,128)(2,1)S(1)}, bf16[160,768]{1,0:T(8,128)(2,1)S(1)}, u32[]{:S(2)}, u32[]{:S(2)}) collective-permute-start(bf16[160,768]{1,0:T(8,128)(2,1)S(1)} %collective-permute-done.9.refs_4_), channel_id=1, source_target_pairs={{0,224},{16,240},{32,0},{48,16},{64,32},{80,48},{96,64},{112,80},{... | collective-permute-start | bytes 737288 | tf_op jit(solution)/shard_map/cond/branch_1_fun/ppermute | solution.py:392
  87.7 3.2 %collective-permute-done.10.refs_5_ = bf16[160,768]{1,0:T(8,128)(2,1)S(1)} collective-permute-done((bf16[160,768]{1,0:T(8,128)(2,1)S(1)}, bf16[160,768]{1,0:T(8,128)(2,1)S(1)}, u32[]{:S(2)}, u32[]{:S(2)}) %collective-permute-start.10) | collective-permute-done | bytes 245792 | tf_op jit(solution)/shard_map/cond/branch_1_fun/ppermute | solution.py:392
  91.1 2.9 %collective-permute-start.13 = (bf16[80,768]{1,0:T(8,128)(2,1)S(1)}, bf16[80,768]{1,0:T(8,128)(2,1)S(1)}, u32[]{:S(2)}, u32[]{:S(2)}) collective-permute-start(bf16[80,768]{1,0:T(8,128)(2,1)S(1)} %slice.95), channel_id=1, source_target_pairs={{0,224},{16,240},{32,0},{48,16},{64,32},{80,48},{96,64},{112,80},{... | collective-permute-start | bytes 368648 | tf_op jit(solution)/shard_map/cond/branch_1_fun/ppermute | solution.py:392
  94.1 9.7 %branch_1_fun.7 = (f32[1024,256]{1,0:T(8,128)S(1)}, f32[1024,512]{1,0:T(8,128)}) custom-call(s32[2,3]{1,0:T(2,128)S(1)} %get-tuple-element.60.live, bf16[1024,256]{1,0:T(8,128)(2,1)} %get-tuple-element.34.q, bf16[1024,256]{1,0:T(8,128)(2,1)} %get-tuple-element.37.k, bf16[1024,256]{1,0:T(8,128)(2,1)} %get-tuple-element.38.v, ...), custom_call_target="tpu_custom_call" | custom-call | tf_op jit(solution)/shard_map/cond/branch_1_fun/pallas_call | solution.py:23
  103.8 9.3 %branch_1_fun.8 = (bf16[1024,256]{1,0:T(8,128)(2,1)S(1)}, bf16[1024,256]{1,0:T(8,128)(2,1)S(1)}) custom-call(s32[16]{0:T(128)S(1)} %fusion.84.places, bf16[1024,256]{1,0:T(8,128)(2,1)} %get-tuple-element.34.q, f32[2,1,1024]{2,1,0:T(1,128)S(1)} %select_n.221.bias, f32[1024,256]{1,0:T(8,128)S(1)} %get-tuple-element.41.acc, ...), custom_call_target="tpu_custom_call" | custom-call | tf_op jit(solution)/shard_map/cond/branch_1_fun/pallas_call | solution.py:23
  113.1 5.8 %branch_1_fun.9 = bf16[1024,384]{1,0:T(8,128)(2,1)} custom-call(bf16[1024,256]{1,0:T(8,128)(2,1)S(1)} %get-tuple-element.48.qg, bf16[1024,256]{1,0:T(8,128)(2,1)S(1)} %copy-done.1, bf16[1024,256]{1,0:T(8,128)(2,1)S(1)} %copy-done.4), custom_call_target="tpu_custom_call" | custom-call | tf_op jit(solution)/shard_map/cond/branch_1_fun/pallas_call | solution.py:23
  118.9 4.7 %all-to-all-start = ((bf16[16,64,384]{2,1,0:T(8,128)(2,1)}), bf16[16,64,384]{2,1,0:T(8,128)(2,1)S(1)}, u32[]{:S(2)}, u32[]{:S(2)}) async-start(bf16[16,64,384]{2,1,0:T(8,128)(2,1)} %bitcast.68), calls=%async_computation | async-start | bytes 1572864 | tf_op jit(solution)/shard_map/cond/branch_1_fun/all_to_all | solution.py:499
  123.7 2.5 %copy.117 = bf16[32,8,8,512]{3,2,1,0:T(8,128)(2,1)S(1)} copy(bf16[32,8,8,512]{3,1,2,0:T(8,128)(2,1)} %bitcast.203) | data formatting | bytes 4194304 | tf_op jit(solution)/shard_map/cond
  126.7 5.1 %constant_dynamic-slice_fusion.8 = (bf16[256,1,512]{2,1,0:T(2,128)(2,1)S(1)}, bf16[256,1,512]{2,1,0:T(2,128)(2,1)S(1)}, bf16[256,1,512]{2,1,0:T(2,128)(2,1)S(1)}...) fusion(bf16[256,8,512]{2,1,0:T(8,128)(2,1)S(1)} %bitcast.199, ...), kind=kLoop, calls=%fused_computation.151 | loop fusion | bytes 4194336 | tf_op jit(solution)/shard_map/cond/branch_1_fun/jit(dynamic_index_in_dim)/dynamic_slice | solution.py:451
  133.1 2.5 %collective-permute-start.31 = (bf16[256,512]{1,0:T(8,128)(2,1)S(1)}, bf16[256,512]{1,0:T(8,128)(2,1)S(1)}, u32[]{:S(2)}, u32[]{:S(2)}) collective-permute-start(bf16[256,512]{1,0:T(8,128)(2,1)S(1)} %bitcast.223), channel_id=1, source_target_pairs={{0,8},{1,9},{2,10},{3,11},{4,12},{5,13},{6,14},{7,15},{8,0},{9,1},... | collective-permute-start | bytes 786440 | tf_op jit(solution)/shard_map/cond/branch_1_fun/ppermute | solution.py:395
  140.0 4.9 %collective-permute-done.18.refs_6_ = bf16[1024,256]{1,0:T(8,128)(2,1)S(1)} collective-permute-done((bf16[1024,256]{1,0:T(8,128)(2,1)S(1)}, bf16[1024,256]{1,0:T(8,128)(2,1)S(1)}, u32[]{:S(2)}, u32[]{:S(2)}) %collective-permute-start.18) | collective-permute-done | bytes 524320 | tf_op jit(solution)/shard_map/cond/branch_1_fun/ppermute | solution.py:395
  147.9 3.9 %collective-permute-done.33.refs_23_ = bf16[256,512]{1,0:T(8,128)(2,1)S(1)} collective-permute-done((bf16[256,512]{1,0:T(8,128)(2,1)S(1)}, bf16[256,512]{1,0:T(8,128)(2,1)S(1)}, u32[]{:S(2)}, u32[]{:S(2)}) %collective-permute-start.33) | collective-permute-done | bytes 262176 | tf_op jit(solution)/shard_map/cond/branch_1_fun/ppermute | solution.py:395
  152.7 3.7 %collective-permute-done.14.refs_2_ = bf16[1024,256]{1,0:T(8,128)(2,1)S(1)} collective-permute-done((bf16[1024,256]{1,0:T(8,128)(2,1)S(1)}, bf16[1024,256]{1,0:T(8,128)(2,1)S(1)}, u32[]{:S(2)}, u32[]{:S(2)}) %collective-permute-start.14) | collective-permute-done | bytes 524320 | tf_op jit(solution)/shard_map/cond/branch_1_fun/ppermute | solution.py:395
  159.2 8.5 %collective-permute-done.19.refs_7_ = bf16[1024,256]{1,0:T(8,128)(2,1)S(1)} collective-permute-done((bf16[1024,256]{1,0:T(8,128)(2,1)S(1)}, bf16[1024,256]{1,0:T(8,128)(2,1)S(1)}, u32[]{:S(2)}, u32[]{:S(2)}) %collective-permute-start.19) | collective-permute-done | bytes 524320 | tf_op jit(solution)/shard_map/cond/branch_1_fun/ppermute | solution.py:395
  169.2 8.3 %collective-permute-done.34.refs_24_ = bf16[256,512]{1,0:T(8,128)(2,1)S(1)} collective-permute-done((bf16[256,512]{1,0:T(8,128)(2,1)S(1)}, bf16[256,512]{1,0:T(8,128)(2,1)S(1)}, u32[]{:S(2)}, u32[]{:S(2)}) %collective-permute-start.34) | collective-permute-done | bytes 262176 | tf_op jit(solution)/shard_map/cond/branch_1_fun/ppermute | solution.py:395
  186.3 4.3 %collective-permute-done.21.refs_9_ = bf16[512,256]{1,0:T(8,128)(2,1)} collective-permute-done((bf16[512,256]{1,0:T(8,128)(2,1)}, bf16[512,256]{1,0:T(8,128)(2,1)}, u32[]{:S(2)}, u32[]{:S(2)}) %collective-permute-start.21) | collective-permute-done | bytes 262176 | tf_op jit(solution)/shard_map/cond/branch_1_fun/ppermute | solution.py:395
  192.4 2.7 %collective-permute-start.29 = (bf16[64,256]{1,0:T(8,128)(2,1)S(1)}, bf16[64,256]{1,0:T(8,128)(2,1)S(1)}, u32[]{:S(2)}, u32[]{:S(2)}) collective-permute-start(bf16[64,256]{1,0:T(8,128)(2,1)S(1)} %collective-permute-done.26.refs_15_), channel_id=1, source_target_pairs={{0,12},{1,13},{2,14},{3,15},{4,0},{5,1},{6,2},{7,3},{8,4},{9,5},{1... | collective-permute-start | bytes 98312 | tf_op jit(solution)/shard_map/cond/branch_1_fun/ppermute | solution.py:395
  197.0 5.8 %branch_1_fun.11 = (f32[1088,256]{1,0:T(8,128)}, f32[1088,256]{1,0:T(8,128)}) custom-call(s32[1]{0:T(128)} %bitcast.32.refs_0_, bf16[1024,256]{1,0:T(8,128)(2,1)S(1)} %get-tuple-element.47.refs_1_, bf16[1024,256]{1,0:T(8,128)(2,1)} %copy-done.9, bf16[1024,256]{1,0:T(8,128)(2,1)} %copy-done.10, bf16[512,256]{1,0:T(8,128)(2,1)S(1)} %collective-permute-done.16.refs_4_, ...), custom_call_target="tpu_custom_call" | custom-call | tf_op jit(solution)/shard_map/cond/branch_1_fun/pallas_call | solution.py:23
  202.8 4.8 %collective-permute-start.37 = (f32[1088,256]{1,0:T(8,128)}, f32[1088,256]{1,0:T(8,128)S(1)}, u32[]{:S(2)}, u32[]{:S(2)}) collective-permute-start(f32[1088,256]{1,0:T(8,128)} %get-tuple-element.51), channel_id=1, source_target_pairs={{0,1},{1,0},{2,3},{3,2},{4,5},{5,4},{6,7},{7,6},{8,9},{9,8},{10,11... | collective-permute-start | bytes 3342344 | tf_op jit(solution)/shard_map/cond/branch_1_fun/ppermute | solution.py:395
  207.6 2.6 %collective-permute-done.37 = f32[1088,256]{1,0:T(8,128)S(1)} collective-permute-done((f32[1088,256]{1,0:T(8,128)}, f32[1088,256]{1,0:T(8,128)S(1)}, u32[]{:S(2)}, u32[]{:S(2)}) %collective-permute-start.37) | collective-permute-done | bytes 1114144 | tf_op jit(solution)/shard_map/cond/branch_1_fun/ppermute | solution.py:395
  210.2 2.2 add_convert_fusion
  (120 shorter events, 38.2 us)
Async XLA Ops:
  27.8 13.2 %collective-permute-start.2 = (bf16[80,768]{1,0:T(8,128)(2,1)S(1)}, bf16[80,768]{1,0:T(8,128)(2,1)S(1)}, u32[]{:S(2)}, u32[]{:S(2)}) collective-permute-start(bf16[80,768]{1,0:T(8,128)(2,1)S(1)} %get-tuple-element.44), channel_id=1, source_target_pairs={{0,16},{16,0},{32,48},{48,32},{64,80},{80,64},{96,112},{112,96},{1... | collective-permute-start | bytes 368648 | tf_op jit(solution)/shard_map/cond/branch_1_fun/ppermute | solution.py:392
  31.6 9.5 %collective-permute-start.3 = (bf16[80,768]{1,0:T(8,128)(2,1)S(1)}, bf16[80,768]{1,0:T(8,128)(2,1)S(1)}, u32[]{:S(2)}, u32[]{:S(2)}) collective-permute-start(bf16[80,768]{1,0:T(8,128)(2,1)S(1)} %get-tuple-element.45), channel_id=1, source_target_pairs={{0,32},{16,48},{32,0},{48,16},{64,96},{80,112},{96,64},{112,80},{1... | collective-permute-start | bytes 368648 | tf_op jit(solution)/shard_map/cond/branch_1_fun/ppermute | solution.py:392
  33.2 7.8 %collective-permute-start.4 = (bf16[80,768]{1,0:T(8,128)(2,1)S(1)}, bf16[80,768]{1,0:T(8,128)(2,1)S(1)}, u32[]{:S(2)}, u32[]{:S(2)}) collective-permute-start(bf16[80,768]{1,0:T(8,128)(2,1)S(1)} %get-tuple-element.46), channel_id=1, source_target_pairs={{0,48},{16,32},{32,16},{48,0},{64,112},{80,96},{96,80},{112,64},{1... | collective-permute-start | bytes 368648 | tf_op jit(solution)/shard_map/cond/branch_1_fun/ppermute | solution.py:392
  33.2 60.9 %collective-permute-start = (bf16[512,512]{1,0:T(8,128)(2,1)}, bf16[512,512]{1,0:T(8,128)(2,1)S(1)}, u32[]{:S(2)}, u32[]{:S(2)}) collective-permute-start(bf16[512,512]{1,0:T(8,128)(2,1)} %get-tuple-element.39), channel_id=1, source_target_pairs={{0,16},{16,32},{32,48},{48,64},{64,80},{80,96},{96,112},{112,128},... | collective-permute-start | bytes 1572872 | tf_op jit(solution)/shard_map/cond/branch_1_fun/ppermute | solution.py:392
  35.9 58.2 %collective-permute-start.1 = (bf16[512,512]{1,0:T(8,128)(2,1)S(1)}, bf16[512,512]{1,0:T(8,128)(2,1)S(1)}, u32[]{:S(2)}, u32[]{:S(2)}) collective-permute-start(bf16[512,512]{1,0:T(8,128)(2,1)S(1)} %get-tuple-element.40), channel_id=1, source_target_pairs={{0,240},{16,0},{32,16},{48,32},{64,48},{80,64},{96,80},{112,96},{1... | collective-permute-start | bytes 1572872 | tf_op jit(solution)/shard_map/cond/branch_1_fun/ppermute | solution.py:392
  41.1 24.4 %collective-permute-start.5 = (bf16[80,768]{1,0:T(8,128)(2,1)S(1)}, bf16[80,768]{1,0:T(8,128)(2,1)S(1)}, u32[]{:S(2)}, u32[]{:S(2)}) collective-permute-start(bf16[80,768]{1,0:T(8,128)(2,1)S(1)} %add_add_fusion), channel_id=1, source_target_pairs={{0,16},{16,0},{32,48},{48,32},{64,80},{80,64},{96,112},{112,96},{1... | collective-permute-start | bytes 368648 | tf_op jit(solution)/shard_map/cond/branch_1_fun/ppermute | solution.py:392
  65.5 11.1 %collective-permute-start.6 = (bf16[160,768]{1,0:T(8,128)(2,1)S(1)}, bf16[160,768]{1,0:T(8,128)(2,1)S(1)}, u32[]{:S(2)}, u32[]{:S(2)}) collective-permute-start(bf16[160,768]{1,0:T(8,128)(2,1)S(1)} %pad_maximum_fusion.2.refs_0_), channel_id=1, source_target_pairs={{0,32},{16,48},{32,64},{48,80},{64,96},{80,112},{96,128},{112,144}... | collective-permute-start | bytes 737288 | tf_op jit(solution)/shard_map/cond/branch_1_fun/ppermute | solution.py:392
  66.2 10.4 %collective-permute-start.7 = (bf16[160,768]{1,0:T(8,128)(2,1)S(1)}, bf16[160,768]{1,0:T(8,128)(2,1)S(1)}, u32[]{:S(2)}, u32[]{:S(2)}) collective-permute-start(bf16[160,768]{1,0:T(8,128)(2,1)S(1)} %pad_maximum_fusion.2.refs_0_), channel_id=1, source_target_pairs={{0,224},{16,240},{32,0},{48,16},{64,32},{80,48},{96,64},{112,80},{... | collective-permute-start | bytes 737288 | tf_op jit(solution)/shard_map/cond/branch_1_fun/ppermute | solution.py:392
  76.6 7.6 %collective-permute-start.8 = (bf16[160,768]{1,0:T(8,128)(2,1)S(1)}, bf16[160,768]{1,0:T(8,128)(2,1)S(1)}, u32[]{:S(2)}, u32[]{:S(2)}) collective-permute-start(bf16[160,768]{1,0:T(8,128)(2,1)S(1)} %collective-permute-done.6.refs_1_), channel_id=1, source_target_pairs={{0,32},{16,48},{32,64},{48,80},{64,96},{80,112},{96,128},{112,144}... | collective-permute-start | bytes 737288 | tf_op jit(solution)/shard_map/cond/branch_1_fun/ppermute | solution.py:392
  76.6 7.6 %collective-permute-start.9 = (bf16[160,768]{1,0:T(8,128)(2,1)S(1)}, bf16[160,768]{1,0:T(8,128)(2,1)S(1)}, u32[]{:S(2)}, u32[]{:S(2)}) collective-permute-start(bf16[160,768]{1,0:T(8,128)(2,1)S(1)} %collective-permute-done.7.refs_2_), channel_id=1, source_target_pairs={{0,224},{16,240},{32,0},{48,16},{64,32},{80,48},{96,64},{112,80},{... | collective-permute-start | bytes 737288 | tf_op jit(solution)/shard_map/cond/branch_1_fun/ppermute | solution.py:392
  84.3 6.8 %collective-permute-start.11 = (bf16[160,768]{1,0:T(8,128)(2,1)S(1)}, bf16[160,768]{1,0:T(8,128)(2,1)S(1)}, u32[]{:S(2)}, u32[]{:S(2)}) collective-permute-start(bf16[160,768]{1,0:T(8,128)(2,1)S(1)} %collective-permute-done.9.refs_4_), channel_id=1, source_target_pairs={{0,224},{16,240},{32,0},{48,16},{64,32},{80,48},{96,64},{112,80},{... | collective-permute-start | bytes 737288 | tf_op jit(solution)/shard_map/cond/branch_1_fun/ppermute | solution.py:392
  91.0 12.8 %collective-permute-start.12 = (bf16[80,768]{1,0:T(8,128)(2,1)S(1)}, bf16[80,768]{1,0:T(8,128)(2,1)S(1)}, u32[]{:S(2)}, u32[]{:S(2)}) collective-permute-start(bf16[80,768]{1,0:T(8,128)(2,1)S(1)} %slice.94), channel_id=1, source_target_pairs={{0,32},{16,48},{32,64},{48,80},{64,96},{80,112},{96,128},{112,144}... | collective-permute-start | bytes 368648 | tf_op jit(solution)/shard_map/cond/branch_1_fun/ppermute | solution.py:392
  91.1 12.7 %collective-permute-start.13 = (bf16[80,768]{1,0:T(8,128)(2,1)S(1)}, bf16[80,768]{1,0:T(8,128)(2,1)S(1)}, u32[]{:S(2)}, u32[]{:S(2)}) collective-permute-start(bf16[80,768]{1,0:T(8,128)(2,1)S(1)} %slice.95), channel_id=1, source_target_pairs={{0,224},{16,240},{32,0},{48,16},{64,32},{80,48},{96,64},{112,80},{... | collective-permute-start | bytes 368648 | tf_op jit(solution)/shard_map/cond/branch_1_fun/ppermute | solution.py:392
  118.9 62.2 %all-to-all-start = ((bf16[16,64,384]{2,1,0:T(8,128)(2,1)}), bf16[16,64,384]{2,1,0:T(8,128)(2,1)S(1)}, u32[]{:S(2)}, u32[]{:S(2)}) async-start(bf16[16,64,384]{2,1,0:T(8,128)(2,1)} %bitcast.68), calls=%async_computation | async-start | bytes 1572864 | tf_op jit(solution)/shard_map/cond/branch_1_fun/all_to_all | solution.py:499
  126.2 18.7 %collective-permute-start.18 = (bf16[1024,256]{1,0:T(8,128)(2,1)S(1)}, bf16[1024,256]{1,0:T(8,128)(2,1)S(1)}, u32[]{:S(2)}, u32[]{:S(2)}) collective-permute-start(bf16[1024,256]{1,0:T(8,128)(2,1)S(1)} %get-tuple-element.47.refs_1_), channel_id=1, source_target_pairs={{0,2},{1,3},{2,0},{3,1},{4,6},{5,7},{6,4},{7,5},{8,10},{9,11},{10,... | collective-permute-start | bytes 1572872 | tf_op jit(solution)/shard_map/cond/branch_1_fun/ppermute | solution.py:395
  133.1 13.0 %collective-permute-start.31 = (bf16[256,512]{1,0:T(8,128)(2,1)S(1)}, bf16[256,512]{1,0:T(8,128)(2,1)S(1)}, u32[]{:S(2)}, u32[]{:S(2)}) collective-permute-start(bf16[256,512]{1,0:T(8,128)(2,1)S(1)} %bitcast.223), channel_id=1, source_target_pairs={{0,8},{1,9},{2,10},{3,11},{4,12},{5,13},{6,14},{7,15},{8,0},{9,1},... | collective-permute-start | bytes 786440 | tf_op jit(solution)/shard_map/cond/branch_1_fun/ppermute | solution.py:395
  135.7 10.6 %collective-permute-start.32 = (bf16[256,512]{1,0:T(8,128)(2,1)S(1)}, bf16[256,512]{1,0:T(8,128)(2,1)S(1)}, u32[]{:S(2)}, u32[]{:S(2)}) collective-permute-start(bf16[256,512]{1,0:T(8,128)(2,1)S(1)} %bitcast.222), channel_id=1, source_target_pairs={{0,12},{1,13},{2,14},{3,15},{4,0},{5,1},{6,2},{7,3},{8,4},{9,5},{1... | collective-permute-start | bytes 786440 | tf_op jit(solution)/shard_map/cond/branch_1_fun/ppermute | solution.py:395
  137.3 19.1 %collective-permute-start.14 = (bf16[1024,256]{1,0:T(8,128)(2,1)S(1)}, bf16[1024,256]{1,0:T(8,128)(2,1)S(1)}, u32[]{:S(2)}, u32[]{:S(2)}) collective-permute-start(bf16[1024,256]{1,0:T(8,128)(2,1)S(1)} %get-tuple-element.47.refs_1_), channel_id=1, source_target_pairs={{0,4},{1,5},{2,6},{3,7},{4,8},{5,9},{6,10},{7,11},{8,12},{9,13},{1... | collective-permute-start | bytes 1572872 | tf_op jit(solution)/shard_map/cond/branch_1_fun/ppermute | solution.py:395
  138.6 19.9 %collective-permute-start.15 = (bf16[1024,256]{1,0:T(8,128)(2,1)S(1)}, bf16[1024,256]{1,0:T(8,128)(2,1)S(1)}, u32[]{:S(2)}, u32[]{:S(2)}) collective-permute-start(bf16[1024,256]{1,0:T(8,128)(2,1)S(1)} %get-tuple-element.47.refs_1_), channel_id=1, source_target_pairs={{0,12},{1,13},{2,14},{3,15},{4,0},{5,1},{6,2},{7,3},{8,4},{9,5},{1... | collective-permute-start | bytes 1572872 | tf_op jit(solution)/shard_map/cond/branch_1_fun/ppermute | solution.py:395
  144.9 22.8 %collective-permute-start.19 = (bf16[1024,256]{1,0:T(8,128)(2,1)S(1)}, bf16[1024,256]{1,0:T(8,128)(2,1)S(1)}, u32[]{:S(2)}, u32[]{:S(2)}) collective-permute-start(bf16[1024,256]{1,0:T(8,128)(2,1)S(1)} %collective-permute-done.18.refs_6_), channel_id=1, source_target_pairs={{0,4},{1,5},{2,6},{3,7},{4,8},{5,9},{6,10},{7,11},{8,12},{9,13},{1... | collective-permute-start | bytes 1572872 | tf_op jit(solution)/shard_map/cond/branch_1_fun/ppermute | solution.py:395
  146.3 31.2 %collective-permute-start.20 = (bf16[1024,256]{1,0:T(8,128)(2,1)S(1)}, bf16[1024,256]{1,0:T(8,128)(2,1)S(1)}, u32[]{:S(2)}, u32[]{:S(2)}) collective-permute-start(bf16[1024,256]{1,0:T(8,128)(2,1)S(1)} %collective-permute-done.18.refs_6_), channel_id=1, source_target_pairs={{0,12},{1,13},{2,14},{3,15},{4,0},{5,1},{6,2},{7,3},{8,4},{9,5},{1... | collective-permute-start | bytes 1572872 | tf_op jit(solution)/shard_map/cond/branch_1_fun/ppermute | solution.py:395
  151.8 25.7 %collective-permute-start.34 = (bf16[256,512]{1,0:T(8,128)(2,1)S(1)}, bf16[256,512]{1,0:T(8,128)(2,1)S(1)}, u32[]{:S(2)}, u32[]{:S(2)}) collective-permute-start(bf16[256,512]{1,0:T(8,128)(2,1)S(1)} %bitcast.221), channel_id=1, source_target_pairs={{0,6},{1,7},{2,4},{3,5},{4,10},{5,11},{6,8},{7,9},{8,14},{9,15},{1... | collective-permute-start | bytes 786440 | tf_op jit(solution)/shard_map/cond/branch_1_fun/ppermute | solution.py:395
  156.5 23.2 %collective-permute-start.35 = (bf16[256,512]{1,0:T(8,128)(2,1)S(1)}, bf16[256,512]{1,0:T(8,128)(2,1)S(1)}, u32[]{:S(2)}, u32[]{:S(2)}) collective-permute-start(bf16[256,512]{1,0:T(8,128)(2,1)S(1)} %bitcast.220), channel_id=1, source_target_pairs={{0,10},{1,11},{2,8},{3,9},{4,14},{5,15},{6,12},{7,13},{8,2},{9,3},... | collective-permute-start | bytes 786440 | tf_op jit(solution)/shard_map/cond/branch_1_fun/ppermute | solution.py:395
  158.5 23.4 %collective-permute-start.36 = (bf16[256,512]{1,0:T(8,128)(2,1)}, bf16[256,512]{1,0:T(8,128)(2,1)S(1)}, u32[]{:S(2)}, u32[]{:S(2)}) collective-permute-start(bf16[256,512]{1,0:T(8,128)(2,1)} %bitcast.186), channel_id=1, source_target_pairs={{0,14},{1,15},{2,12},{3,13},{4,2},{5,3},{6,0},{7,1},{8,6},{9,7},{1... | collective-permute-start | bytes 786440 | tf_op jit(solution)/shard_map/cond/branch_1_fun/ppermute | solution.py:395
  167.7 14.9 %collective-permute-start.16 = (bf16[512,256]{1,0:T(8,128)(2,1)}, bf16[512,256]{1,0:T(8,128)(2,1)S(1)}, u32[]{:S(2)}, u32[]{:S(2)}) collective-permute-start(bf16[512,256]{1,0:T(8,128)(2,1)} %slice.96), channel_id=1, source_target_pairs={{0,4},{1,5},{2,6},{3,7},{4,8},{5,9},{6,10},{7,11},{8,12},{9,13},{1... | collective-permute-start | bytes 786440 | tf_op jit(solution)/shard_map/cond/branch_1_fun/ppermute | solution.py:395
  177.5 7.1 %collective-permute-start.17 = (bf16[512,256]{1,0:T(8,128)(2,1)}, bf16[512,256]{1,0:T(8,128)(2,1)}, u32[]{:S(2)}, u32[]{:S(2)}) collective-permute-start(bf16[512,256]{1,0:T(8,128)(2,1)} %slice.97), channel_id=1, source_target_pairs={{0,12},{1,13},{2,14},{3,15},{4,0},{5,1},{6,2},{7,3},{8,4},{9,5},{1... | collective-permute-start | bytes 786440 | tf_op jit(solution)/shard_map/cond/branch_1_fun/ppermute | solution.py:395
  177.5 13.2 %collective-permute-start.21 = (bf16[512,256]{1,0:T(8,128)(2,1)}, bf16[512,256]{1,0:T(8,128)(2,1)}, u32[]{:S(2)}, u32[]{:S(2)}) collective-permute-start(bf16[512,256]{1,0:T(8,128)(2,1)} %slice.98), channel_id=1, source_target_pairs={{0,4},{1,5},{2,6},{3,7},{4,8},{5,9},{6,10},{7,11},{8,12},{9,13},{1... | collective-permute-start | bytes 786440 | tf_op jit(solution)/shard_map/cond/branch_1_fun/ppermute | solution.py:395
  179.7 12.6 %collective-permute-start.22 = (bf16[512,256]{1,0:T(8,128)(2,1)}, bf16[512,256]{1,0:T(8,128)(2,1)}, u32[]{:S(2)}, u32[]{:S(2)}) collective-permute-start(bf16[512,256]{1,0:T(8,128)(2,1)} %slice.99), channel_id=1, source_target_pairs={{0,12},{1,13},{2,14},{3,15},{4,0},{5,1},{6,2},{7,3},{8,4},{9,5},{1... | collective-permute-start | bytes 786440 | tf_op jit(solution)/shard_map/cond/branch_1_fun/ppermute | solution.py:395
  181.9 8.9 %collective-permute-start.26 = (bf16[64,256]{1,0:T(8,128)(2,1)S(1)}, bf16[64,256]{1,0:T(8,128)(2,1)S(1)}, u32[]{:S(2)}, u32[]{:S(2)}) collective-permute-start(bf16[64,256]{1,0:T(8,128)(2,1)S(1)} %branch_1_fun.10.refs_11_), channel_id=1, source_target_pairs={{0,2},{1,3},{2,0},{3,1},{4,6},{5,7},{6,4},{7,5},{8,10},{9,11},{10,... | collective-permute-start | bytes 98312 | tf_op jit(solution)/shard_map/cond/branch_1_fun/ppermute | solution.py:395
  182.6 9.8 %collective-permute-start.23 = (bf16[64,256]{1,0:T(8,128)(2,1)S(1)}, bf16[64,256]{1,0:T(8,128)(2,1)S(1)}, u32[]{:S(2)}, u32[]{:S(2)}) collective-permute-start(bf16[64,256]{1,0:T(8,128)(2,1)S(1)} %branch_1_fun.10.refs_11_), channel_id=1, source_target_pairs={{0,4},{1,5},{2,6},{3,7},{4,8},{5,9},{6,10},{7,11},{8,12},{9,13},{1... | collective-permute-start | bytes 98312 | tf_op jit(solution)/shard_map/cond/branch_1_fun/ppermute | solution.py:395
  184.6 11.6 %collective-permute-start.24 = (bf16[64,256]{1,0:T(8,128)(2,1)S(1)}, bf16[64,256]{1,0:T(8,128)(2,1)S(1)}, u32[]{:S(2)}, u32[]{:S(2)}) collective-permute-start(bf16[64,256]{1,0:T(8,128)(2,1)S(1)} %branch_1_fun.10.refs_11_), channel_id=1, source_target_pairs={{0,8},{1,9},{2,10},{3,11},{4,12},{5,13},{6,14},{7,15},{8,0},{9,1},... | collective-permute-start | bytes 98312 | tf_op jit(solution)/shard_map/cond/branch_1_fun/ppermute | solution.py:395
  202.8 7.4 %collective-permute-start.37 = (f32[1088,256]{1,0:T(8,128)}, f32[1088,256]{1,0:T(8,128)S(1)}, u32[]{:S(2)}, u32[]{:S(2)}) collective-permute-start(f32[1088,256]{1,0:T(8,128)} %get-tuple-element.51), channel_id=1, source_target_pairs={{0,1},{1,0},{2,3},{3,2},{4,5},{5,4},{6,7},{7,6},{8,9},{9,8},{10,11... | collective-permute-start | bytes 3342344 | tf_op jit(solution)/shard_map/cond/branch_1_fun/ppermute | solution.py:395
  (16 other events, 252.3 us)
